TPU v7x, 256 devices: a whole 4x4x8 slice. The times are simulated.
256 devices in a mesh: frame: 16 (over z_lo, y), patch: 16 (over z_hi, x, core).
Axes of the slice: x: 4, y: 4, z: 8 (z_hi: 2, z_lo: 4; z = z_hi * 4 + z_lo), core: 2. Of those that a mesh axis runs over, the one named last changes fastest.
Arguments:
- hidden_states: bfloat16 [16, 4096, 1152], P('frame', 'patch'), may hold values from -6 to 6
- mod_spatial: float32 [3, 1152], replicated, may hold values from -4 to 4
- w_spatial_qkv: bfloat16 [1152, 3456], P(None, 'patch'), may hold values from -2.5 to 2.5
- w_spatial_out: bfloat16 [1152, 1152], P('patch'), may hold values from -0.1875 to 0.1875
- mod_temporal: float32 [3, 1152], replicated, may hold values from -4 to 4
- w_temporal_qkv: bfloat16 [1152, 3456], P(None, 'frame'), may hold values from -2.5 to 2.5
- w_temporal_out: bfloat16 [1152, 1152], P('frame'), may hold values from -0.1875 to 0.1875
Outputs:
- block_out: bfloat16 [16, 4096, 1152], P('frame', 'patch')
All inputs are finite; a program needn't handle non-finite values.
Results may differ from a plain program's by a relative error of at most 0.017.
Values may be sent and summed in bfloat16 or wider, within the bound.
A program may use at most 64 MiB of HBM per device.

v0:
```python
import functools
import math

import jax
import jax.numpy as jnp
from jax import lax
from jax.experimental import pallas as pl
from jax.experimental.pallas import tpu as pltpu
from jax.sharding import PartitionSpec as P

HEADS = 16
HEAD_DIM = 72
EPS = 1e-06
MESH = pl.DeviceIdType.MESH
Q_SCALE = math.log2(math.e) / math.sqrt(HEAD_DIM)
LOW = -1e30
N_SEND = 16
N_RECV = 72
Y_ORDER = (0, 3, 1, 2)
SCHEDULE = (
    ("C",), ("S", 0), ("M", 0), ("M", 1), ("Y",), ("F", 0), ("S", 1), ("YF", 0),
    ("CS",), ("Z", 0), ("L", 0), ("YL", 0), ("YS", 0), ("Z", 1), ("YS", 1), ("F", 1),
    ("ZS", 0), ("Z", 2), ("L", 1), ("CD",), ("T", 0), ("T", 1), ("F", 2), ("A", 0, 1024, 0),
    ("ZS", 1), ("Z", 3), ("M", 2), ("A", 0, 1024, 512), ("L", 2), ("A", 1024, 1024, 0), ("T", 2), ("F", 3),
    ("A", 1024, 1024, 512), ("ZS", 2), ("YF", 1), ("YF", 2), ("OS",), ("A", 0, 2048, 1024), ("L", 3), ("A", 0, 2048, 1536),
    ("ZS", 3), ("T", 3), ("F", 4), ("A", 0, 2048, 2048), ("YS", 2), ("YL", 1), ("YL", 2), ("A", 0, 2048, 2560),
    ("L", 4), ("T", 4), ("F", 5), ("OF",), ("A", 0, 2048, 3072), ("YF", 3), ("L", 5), ("T", 5),
    ("OL",), ("A", 0, 2048, 3584),
)
TAIL = (
    ("YL", 3),
)


def dot(a, b, ca, cb):
    return lax.dot_general(a, b, (((ca,), (cb,)), ((), ())), preferred_element_type=jnp.float32)


def modulate(tokens, mod_ref):
    values = tokens.astype(jnp.float32)
    mean = jnp.mean(values, axis=-1, keepdims=True)
    centred = values - mean
    var = jnp.mean(centred * centred, axis=-1, keepdims=True)
    normed = centred * lax.rsqrt(var + EPS)
    return (normed * (1.0 + mod_ref[1:2, :]) + mod_ref[0:1, :]).astype(jnp.bfloat16)


def kernel(
    hid_ref, mod_s_ref, mod_t_ref, ws_qkv_ref, ws_out_ref, wt_qkv_ref, wt_out_ref, out_ref,
    tok_a, tok_b, wsp, wso, wt, wto, q_buf, k_buf, v_buf, acc, top, o_send, o_recv,
    t_send, t_recv, r_send, heads_t, moved_t, send_sem, recv_sem,
):
    frame = lax.axis_index("frame")
    patch = lax.axis_index("patch")
    zlo, y = frame // 4, lax.rem(frame, 4)
    zhi, x, c = patch // 8, lax.rem(patch // 2, 4), lax.rem(patch, 2)
    z = zhi * 4 + zlo
    slot = x * 2 + c

    def device(z_=z, y_=y, x_=x, c_=c):
        return (lax.rem(z_, 4) * 4 + y_, (z_ // 4) * 8 + x_ * 2 + c_)

    def turn(value, step, size):
        return lax.rem(value + step + size, size)

    right, left = device(x_=turn(x, 1, 4)), device(x_=turn(x, -1, 4))
    sibling = device(c_=1 - c)
    partner = device(z_=turn(z, 4, 8))
    x_slots = [turn(x, d, 4) * 2 + c for d in range(4)]
    sib_slots = [turn(x, d, 4) * 2 + 1 - c for d in range(4)]

    barrier = pltpu.get_barrier_semaphore()
    greet = [device(x_=turn(x, d // 2, 4), c_=turn(c, d % 2, 2)) for d in range(1, 8)]
    greet += [(turn(frame, d, 16), patch) for d in range(1, 16)]
    greet += [device(z_=turn(z, d, 8)) for d in (4, 1, -1, 2, -2)]
    for other in greet:
        pl.semaphore_signal(barrier, inc=1, device_id=other, device_id_type=MESH)

    send_ids, recv_ids, fresh = {}, {}, [0]

    class Move:
        def __init__(self, src, dst, target, landing, group, recv_group=None):
            self.s = send_ids.setdefault(group, len(send_ids))
            if recv_group is None:
                fresh[0] += 1
                recv_group = fresh[0]
            self.r = recv_ids.setdefault(recv_group, len(recv_ids))
            self.src, self.dst, self.target, self.landing = src, dst, target, landing

        def start(self):
            pltpu.make_async_remote_copy(
                src_ref=self.src, dst_ref=self.dst, send_sem=send_sem.at[self.s],
                recv_sem=recv_sem.at[self.r], device_id=self.target, device_id_type=MESH,
            ).start()

        def wait_recv(self, landing=None):
            landing = self.landing if landing is None else landing
            pltpu.make_async_remote_copy(
                src_ref=landing, dst_ref=landing, send_sem=send_sem.at[self.s],
                recv_sem=recv_sem.at[self.r], device_id=self.target, device_id_type=MESH,
            ).wait_recv()

    def sent(group, ref):
        i = send_ids[group]
        pltpu.make_async_remote_copy(
            src_ref=ref, dst_ref=ref, send_sem=send_sem.at[i],
            recv_sem=recv_sem.at[0], device_id=sibling, device_id_type=MESH,
        ).wait_send()

    def start(*moves):
        for m in moves:
            m.start()

    def recv(*moves):
        for m in moves:
            m.wait_recv()

    class Ring:
        def __init__(self, buf, rows, cut, group, name):
            me, near, far, back = [buf.at[s] for s in x_slots]
            self.buf = buf
            self.to_right = Move(me, me, right, back, group)
            self.to_left = Move(me, me, left, near, group)
            top_half, low_half = pl.ds(0, cut), pl.ds(cut, rows - cut)
            self.on_right = Move(back.at[top_half], back.at[top_half], right, far.at[top_half], group)
            self.on_left = Move(near.at[low_half], near.at[low_half], left, far.at[low_half], group)
            self.sib = [
                Move(buf.at[x_slots[d]], buf.at[x_slots[d]], sibling, None, group, ("sib", name)) for d in range(4)
            ]

        def begin(self):
            start(self.to_right, self.to_left, self.sib[0])

        def forward(self):
            recv(self.to_right)
            start(self.on_right)
            recv(self.to_left)
            start(self.on_left, self.sib[3], self.sib[1])

        def last(self):
            recv(self.on_right, self.on_left)
            start(self.sib[2])

        def done(self):
            self.sib[0].wait_recv(self.buf.at[0:4])

    rings = [Ring(tok_a.at[n], 128, 64, "near", n) for n in range(2)]
    rings += [Ring(tok_b.at[n], 64, 32, "far", n + 2) for n in range(4)]
    to_partner = [
        Move(tok_a.at[n // 2, slot, pl.ds((n % 2) * 64, 64)], tok_b.at[n, slot], partner, tok_b.at[n, slot], "z")
        for n in range(4)
    ]
    wso_ring = Ring(wso, 144, 64, "wso", 6)

    edge = jnp.logical_or(zlo == 0, zlo == 3)
    ahead = jnp.where(zlo == 0, -1, 1)
    cross_src = wsp.at[0, y]
    cross_dst = wsp.at[1, y]
    cross_near = Move(cross_src, cross_dst, device(z_=turn(z, ahead, 8)), cross_dst, "c1", "cross")
    cross_far = Move(cross_src, cross_dst, device(z_=turn(z, 2 * ahead, 8)), cross_dst, "c2", "cross")
    share = [Move(cross_dst, cross_dst, device(y_=turn(y, d, 4)), None, "share", "share") for d in (1, 3, 2)]

    def wt_slot(dz, dy):
        return turn(zlo, dz, 4) * 4 + turn(y, dy, 4)

    def wt_half(dz, dy):
        return wt.at[wt_slot(dz, dy), c]

    two = jnp.where(c == 0, 2, -2)
    z_moves = [
        Move(wt_half(0, 0), wt_half(0, 0), device(z_=turn(z, 1, 8)), wt_half(-1, 0), "zw"),
        Move(wt_half(0, 0), wt_half(0, 0), device(z_=turn(z, -1, 8)), wt_half(1, 0), "zw"),
        Move(wt_half(0, 0), wt_half(0, 0), device(z_=turn(z, two, 8)), wt_half(2, 0), "zw"),
    ]
    y_up, y_down = device(y_=turn(y, 1, 4)), device(y_=turn(y, -1, 4))

    class YRing:
        def __init__(self, dz):
            me, near, far, back = [wt_half(dz, d) for d in range(4)]
            self.up = Move(me, me, y_up, back, "y")
            self.down = Move(me, me, y_down, near, "y")
            first, second = pl.ds(0, 64), pl.ds(64, 80)
            self.on_up = Move(back.at[first], back.at[first], y_up, far.at[first], "y")
            self.on_down = Move(near.at[second], near.at[second], y_down, far.at[second], "y")
            self.sib = [
                Move(wt_half(dz, d), wt_half(dz, d), sibling, None, "ysib", "ysib")
                for d in range(4) if (dz, d) != (0, 0)
            ]

        def begin(self):
            start(self.up, self.down)
            if len(self.sib) == 4:
                start(self.sib[0])

        def forward(self):
            recv(self.up)
            start(self.on_up)
            recv(self.down)
            start(self.on_down, self.sib[-1], self.sib[-3])

        def last(self):
            recv(self.on_up, self.on_down)
            start(self.sib[-2])

    y_rings = {dz: YRing(dz) for dz in Y_ORDER}

    def project(heads, ref, q_at, k_at):
        tokens = ref[...].reshape(-1, 1152)
        n = tokens.shape[0]
        for h in heads:
            qkv = dot(wsp[h].reshape(320, 1152)[0:224], tokens, 1, 1)
            if q_at is not None:
                q = jnp.concatenate([qkv[0:72] * Q_SCALE, jnp.zeros((8, n), jnp.float32)], axis=0)
                q_buf[h, :, pl.ds(q_at, n)] = q.astype(jnp.bfloat16)
            k = jnp.concatenate([qkv[72:144], jnp.zeros((8, n), jnp.float32)], axis=0)
            k_buf[h, pl.ds(k_at, n), :] = k.T.astype(jnp.bfloat16)
            row = lax.broadcasted_iota(jnp.int32, (8, n), 0)
            one = jnp.where(row == 0, 1.0, 0.0)
            v_buf[h, :, pl.ds(k_at, n)] = jnp.concatenate([qkv[144:216], one], axis=0).astype(jnp.bfloat16)

    def flash(h, q_at, q_n, k_at, k_n):
        qs, ks = pl.ds(q_at, q_n), pl.ds(k_at, k_n)
        s = dot(k_buf[h, ks, :], q_buf[h, :, qs], 1, 0)
        before = top[h, 0:1, qs]
        now = jnp.maximum(before, jnp.max(s, axis=0, keepdims=True))
        p = jnp.exp2(s - now).astype(jnp.bfloat16)
        acc[h, :, qs] = acc[h, :, qs] * jnp.exp2(before - now) + dot(v_buf[h, :, ks], p, 1, 0)
        top[h, 0:1, qs] = now

    moved = modulate(hid_ref[...], mod_s_ref)
    tok_a[0, slot] = moved[0:128]
    tok_a[1, slot] = moved[128:256]
    f32 = jnp.float32
    own = [ws_qkv_ref[...].astype(f32), ws_out_ref[...].astype(f32), jnp.zeros((32, 1152), f32)]
    wsp[0] = jnp.concatenate(own, axis=0).astype(jnp.bfloat16).reshape(4, 80, 1152)
    own = [wt_qkv_ref[...].astype(f32), wt_out_ref[...].astype(f32)]
    wt[frame] = jnp.concatenate(own, axis=0).astype(jnp.bfloat16).reshape(2, 144, 1152)
    acc[...] = jnp.zeros_like(acc)
    top[...] = jnp.full_like(top, LOW)
    pl.semaphore_wait(barrier, len(greet))

    def cross_start():
        @pl.when(edge)
        def _():
            cross_near.start()
            cross_far.start()

    def cross_share():
        recv(cross_near)
        start(*share)

    def share_done():
        share[0].wait_recv(wsp.at[1, 0:3])
        rows = [wsp[h].reshape(320, 1152)[208:288].astype(jnp.float32)[8:80] for h in range(2)]
        wso[slot] = jnp.concatenate(rows, axis=0).astype(jnp.bfloat16)

    def forward_z(n):
        recv(to_partner[n])
        rings[n + 2].begin()

    def forward_y(i):
        recv(z_moves[i])
        y_rings[Y_ORDER[i + 1]].begin()

    def tokens_done(n):
        rings[n].done()
        project((0, 1), *chunks[n])

    def attend(q_at, q_n, k_at):
        for h in range(2):
            flash(h, q_at, q_n, k_at, 512)

    chunks = [(tok_a.at[n], n * 1024, n * 1024) for n in range(2)]
    chunks += [(tok_b.at[n], None, 2048 + n * 512) for n in range(4)]
    steps = {
        "S": lambda n: rings[n].begin(),
        "F": lambda n: rings[n].forward(),
        "L": lambda n: rings[n].last(),
        "T": tokens_done,
        "A": attend,
        "Z": lambda n: to_partner[n].start(),
        "ZS": forward_z,
        "C": cross_start,
        "CS": cross_share,
        "CD": share_done,
        "M": lambda i: z_moves[i].start(),
        "Y": lambda: y_rings[0].begin(),
        "YS": forward_y,
        "YF": lambda i: y_rings[Y_ORDER[i]].forward(),
        "YL": lambda i: y_rings[Y_ORDER[i]].last(),
        "YD": lambda i: y_rings[Y_ORDER[i]].done(),
        "OS": lambda: wso_ring.begin(),
        "OF": lambda: wso_ring.forward(),
        "OL": lambda: wso_ring.last(),
    }
    for step in SCHEDULE:
        steps[step[0]](*step[1:])

    for s in range(8):
        for h in range(2):
            for n in range(2):
                part = acc[h, :, pl.ds(n * 1024 + s * 128, 128)]
                heads_t[pl.ds(h * 72, 72), pl.ds(n * 128, 128)] = part[0:72] * (1.0 / part[72:73])
        o_send[s] = heads_t[0:144, :].astype(jnp.bfloat16)
    o_moves = []
    for d in range(1, 8):
        to = turn(x, d // 2, 4) * 2 + turn(c, d % 2, 2)
        o_moves.append(
            Move(o_send.at[to], o_recv.at[slot], device(x_=to // 2, c_=lax.rem(to, 2)), None, "o", "o")
        )
    start(*o_moves)
    o_recv[slot] = o_send[slot]
    for step in TAIL:
        steps[step[0]](*step[1:])
    wso_ring.done()
    o_moves[0].wait_recv(o_recv.at[0:7])
    update = dot(o_recv[...].reshape(1152, 256), wso[...].reshape(1152, 1152), 0, 0)
    after = (hid_ref[...].astype(jnp.float32) + mod_s_ref[2:3, :] * update).astype(jnp.bfloat16)
    t_send[...] = after.reshape(16, 16, 1152)

    there = []
    for d in range(1, 16):
        to = turn(frame, d, 16)
        there.append(Move(t_send.at[to], t_recv.at[frame], (to, patch), None, "there", "there"))
    start(*there)
    t_recv[frame] = t_send[frame]
    y_rings[0].sib[0].wait_recv(wt.at[0:15, 0])
    for pair in range(8):
        rows = [wt[2 * pair + k].reshape(288, 1152)[208:288].astype(jnp.float32)[8:80] for k in range(2)]
        wto[pair] = jnp.concatenate(rows, axis=0).astype(jnp.bfloat16)
    there[0].wait_recv(t_recv.at[0:15])
    tokens = t_recv[...].reshape(256, 1152)
    t_moved = modulate(tokens, mod_t_ref)
    key = lax.rem(lax.broadcasted_iota(jnp.int32, (256, 256), 0), 16)
    query = lax.rem(lax.broadcasted_iota(jnp.int32, (256, 256), 1), 16)
    bias = jnp.where(key == query, 0.0, LOW)
    one = jnp.where(lax.broadcasted_iota(jnp.int32, (8, 256), 0) == 0, 1.0, 0.0)
    moved_t[...] = t_moved.astype(f32).T.astype(jnp.bfloat16)

    def four_heads(g, _):
        qkv = dot(wt[pl.ds(4 * g, 4)].reshape(1152, 1152), moved_t[...], 1, 0)
        for i in range(4):
            part = qkv[288 * i:288 * i + 216]
            q = (part[0:72] * Q_SCALE).astype(jnp.bfloat16)
            k = part[72:144].T.astype(jnp.bfloat16)
            v = jnp.concatenate([part[144:216], one], axis=0).astype(jnp.bfloat16)
            s = dot(k, q, 1, 0) + bias
            p = jnp.exp2(s - jnp.max(s, axis=0, keepdims=True)).astype(jnp.bfloat16)
            o = dot(v, p, 1, 0)
            rows = pl.ds(pl.multiple_of((4 * g + i) * 72, 8), 72)
            heads_t[rows, :] = o[0:72] * (1.0 / o[72:73])
        return 0

    lax.fori_loop(0, 4, four_heads, 0)
    update = dot(heads_t[...].astype(jnp.bfloat16), wto[...].reshape(1152, 1152), 0, 0)
    block = tokens.astype(jnp.float32) + mod_t_ref[2:3, :] * update
    r_send[...] = block.astype(jnp.bfloat16).reshape(16, 16, 1152)
    back = []
    for d in range(1, 16):
        to = turn(frame, d, 16)
        back.append(Move(r_send.at[to], out_ref.at[frame], (to, patch), None, "back", "back"))
    start(*back)
    out_ref[frame] = r_send[frame]
    back[0].wait_recv(out_ref.at[0:15])

    sent("near", tok_b.at[0:4, 0:7])
    sent("far", tok_b.at[0:4, 0:7])
    sent("wso", wso.at[0:7])
    sent("z", tok_b.at[0, 0:4])
    sent("share", wsp.at[1, 0:3])
    sent("zw", wso.at[0:3])
    sent("y", wt.at[0:6])
    sent("ysib", wt.at[0:15, 0])
    sent("o", o_recv.at[0:7])
    sent("there", t_recv.at[0:15])
    sent("back", t_recv.at[0:15])

    @pl.when(edge)
    def _():
        sent("c1", cross_src)
        sent("c2", cross_src)

    assert len(send_ids) <= N_SEND and len(recv_ids) <= N_RECV


def shards(hidden, mod_s, w_s_qkv, w_s_out, mod_t, w_t_qkv, w_t_out):
    vmem = pl.BlockSpec(memory_space=pltpu.VMEM)
    bf, f32 = jnp.bfloat16, jnp.float32
    out = pl.pallas_call(
        kernel,
        out_shape=jax.ShapeDtypeStruct((16, 16, 1152), bf),
        in_specs=[vmem] * 7,
        out_specs=vmem,
        scratch_shapes=[
            pltpu.VMEM((2, 8, 128, 1152), bf),
            pltpu.VMEM((4, 8, 64, 1152), bf),
            pltpu.VMEM((2, 4, 80, 1152), bf),
            pltpu.VMEM((8, 144, 1152), bf),
            pltpu.VMEM((16, 2, 144, 1152), bf),
            pltpu.VMEM((8, 144, 1152), bf),
            pltpu.VMEM((2, 80, 2048), bf),
            pltpu.VMEM((2, 4096, 80), bf),
            pltpu.VMEM((2, 80, 4096), bf),
            pltpu.VMEM((2, 80, 2048), f32),
            pltpu.VMEM((2, 8, 2048), f32),
            pltpu.VMEM((8, 144, 256), bf),
            pltpu.VMEM((8, 144, 256), bf),
            pltpu.VMEM((16, 16, 1152), bf),
            pltpu.VMEM((16, 16, 1152), bf),
            pltpu.VMEM((16, 16, 1152), bf),
            pltpu.VMEM((1152, 256), f32),
            pltpu.VMEM((1152, 256), bf),
            pltpu.SemaphoreType.DMA((N_SEND,)),
            pltpu.SemaphoreType.DMA((N_RECV,)),
        ],
        compiler_params=pltpu.CompilerParams(
            collective_id=0, has_side_effects=True, vmem_limit_bytes=62 * 2**20
        ),
        name="st_block",
    )(hidden.reshape(256, 1152), mod_s, mod_t, w_s_qkv.T, w_s_out, w_t_qkv.T, w_t_out)
    return out.reshape(1, 256, 1152)


def solution(mesh):
    in_specs = (
        P("frame", "patch", None),
        P(),
        P(None, "patch"),
        P("patch", None),
        P(),
        P(None, "frame"),
        P("frame", None),
    )
    out_specs = P("frame", "patch", None)
    return jax.shard_map(shards, mesh=mesh, in_specs=in_specs, out_specs=out_specs, check_vma=False)
```

profile of v0, /device:TPU:32, one launch (start us, length us, event | category | flops | bytes accessed | tf_op | source)
XLA Modules:
  0.0 138.4 jit_solution(277074507020271986)
XLA Ops:
  0.0 136.5 %st_block.1 = bf16[16,16,1152]{2,1,0:T(8,128)(2,1)} custom-call(bf16[256,1152]{1,0:T(8,128)(2,1)} %bitcast.5, f32[3,1152]{1,0:T(4,128)} %mod_s_ref.1, f32[3,1152]{1,0:T(4,128)} %mod_t_ref.1, bf16[216,1152]{1,0:T(8,128)(2,1)} %bitcast.6, bf16[72,1152]{1,0:T(8,128)(2,1)} %ws_out_ref.1, bf16[216,1152]{1,0:T(8,128)(2,1)} %bitcast.7, bf16[72,1152]{1,0:T(8,128)(2,1)} %wt_out_ref.1), custom_call_target="tpu_custom_call" | custom-call | tf_op jit(solution)/shard_map/st_block/pallas_call | solution.py:389
  136.5 1.9 %copy.9 = bf16[1,256,1152]{2,1,0:T(8,128)(2,1)} copy(bf16[1,256,1152]{2,1,0:T(8,128)(2,1)} %bitcast.4) | data formatting | bytes 1179648
where the time goes:
time: 139 us; the launch traced here: 138 us
  Pallas kernels  137 us (99%)
  local copies, waits for them, and re-layouts  1.92 us (1%)
    pallas_call x1, Pallas kernels, shards(): pl.pallas_call(kernel, out_shape=jax.ShapeDtypeStruct((16, 16, 1152), bf)...  137 us

commit v1 on v0

--- a/solution.py
+++ b/solution.py
@@ -18,17 +18,21 @@
 N_RECV = 72
 Y_ORDER = (0, 3, 1, 2)
 SCHEDULE = (
-    ("C",), ("S", 0), ("M", 0), ("M", 1), ("Y",), ("F", 0), ("S", 1), ("YF", 0),
-    ("CS",), ("Z", 0), ("L", 0), ("YL", 0), ("YS", 0), ("Z", 1), ("YS", 1), ("F", 1),
-    ("ZS", 0), ("Z", 2), ("L", 1), ("CD",), ("T", 0), ("T", 1), ("F", 2), ("A", 0, 1024, 0),
-    ("ZS", 1), ("Z", 3), ("M", 2), ("A", 0, 1024, 512), ("L", 2), ("A", 1024, 1024, 0), ("T", 2), ("F", 3),
-    ("A", 1024, 1024, 512), ("ZS", 2), ("YF", 1), ("YF", 2), ("OS",), ("A", 0, 2048, 1024), ("L", 3), ("A", 0, 2048, 1536),
-    ("ZS", 3), ("T", 3), ("F", 4), ("A", 0, 2048, 2048), ("YS", 2), ("YL", 1), ("YL", 2), ("A", 0, 2048, 2560),
-    ("L", 4), ("T", 4), ("F", 5), ("OF",), ("A", 0, 2048, 3072), ("YF", 3), ("L", 5), ("T", 5),
-    ("OL",), ("A", 0, 2048, 3584),
+    ("S", 0), ("Z", 1), ("C",), ("S", 1), ("F", 0), ("F", 1), ("Z", 2), ("CS",),
+    ("L", 0), ("L", 1), ("ZS", 1), ("T", 0), ("Z", 0), ("T", 1), ("CD",), ("U", 0),
+    ("ZS", 2), ("A", 0, 1024, 0), ("U", 1), ("OS",), ("A", 0, 1024, 512), ("Z", 3), ("F", 3), ("Y",),
+    ("A", 1024, 1024, 512), ("A", 0, 2048, 1024), ("ZS", 0), ("M", 0), ("A", 0, 2048, 1536), ("L", 3), ("F", 4), ("A", 1024, 1024, 0),
+    ("M", 1), ("F", 2), ("T", 3), ("YF", 0), ("U", 3), ("ZS", 3), ("L", 4), ("A", 0, 2048, 2560),
+    ("T", 4), ("M", 2), ("L", 2), ("U", 4), ("YS", 0), ("F", 5), ("A", 0, 2048, 3072), ("T", 2),
+    ("L", 5), ("OF",), ("YS", 1), ("U", 2), ("A", 0, 2048, 2048), ("T", 5), ("U", 5), ("YS", 2),
+    ("YF", 1),
 )
 TAIL = (
-    ("YL", 3),
+    ("OL",),
+)
+LAST_KEYS = 3584
+LATE = (
+    ("YL", 1), ("YF", 2), ("YL", 0), ("YF", 3), ("YL", 2), ("YL", 3),
 )
 
 
@@ -264,7 +268,7 @@
 
     def tokens_done(n):
         rings[n].done()
-        project((0, 1), *chunks[n])
+        project((0,), *chunks[n])
 
     def attend(q_at, q_n, k_at):
         for h in range(2):
@@ -277,6 +281,7 @@
         "F": lambda n: rings[n].forward(),
         "L": lambda n: rings[n].last(),
         "T": tokens_done,
+        "U": lambda n: project((1,), *chunks[n]),
         "A": attend,
         "Z": lambda n: to_partner[n].start(),
         "ZS": forward_z,
@@ -296,34 +301,56 @@
     for step in SCHEDULE:
         steps[step[0]](*step[1:])
 
-    for s in range(8):
-        for h in range(2):
-            for n in range(2):
+    def heads_back(n):
+        attend(n * 1024, 1024, LAST_KEYS)
+        for s in range(8):
+            pair = []
+            for h in range(2):
                 part = acc[h, :, pl.ds(n * 1024 + s * 128, 128)]
-                heads_t[pl.ds(h * 72, 72), pl.ds(n * 128, 128)] = part[0:72] * (1.0 / part[72:73])
-        o_send[s] = heads_t[0:144, :].astype(jnp.bfloat16)
-    o_moves = []
-    for d in range(1, 8):
-        to = turn(x, d // 2, 4) * 2 + turn(c, d % 2, 2)
-        o_moves.append(
-            Move(o_send.at[to], o_recv.at[slot], device(x_=to // 2, c_=lax.rem(to, 2)), None, "o", "o")
-        )
-    start(*o_moves)
-    o_recv[slot] = o_send[slot]
+                pair.append(part[0:72] * (1.0 / part[72:73]))
+            o_send[n, s] = jnp.concatenate(pair, axis=0).astype(jnp.bfloat16)
+        moves = []
+        for d in range(1, 8):
+            to = turn(x, d // 2, 4) * 2 + turn(c, d % 2, 2)
+            target = device(x_=to // 2, c_=lax.rem(to, 2))
+            moves.append(Move(o_send.at[n, to], o_recv.at[n, slot], target, None, "o", ("o", n)))
+        start(*moves)
+        o_recv[n, slot] = o_send[n, slot]
+        return moves
+
+    my_rows = y * 4 + zlo
+
+    def spatial_end(n, moves):
+        moves[0].wait_recv(o_recv.at[n, 0:7])
+        update = dot(o_recv[n].reshape(1152, 128), wso[...].reshape(1152, 1152), 0, 0)
+        old = hid_ref[pl.ds(n * 128, 128), :].astype(f32)
+        after = (old + mod_s_ref[2:3, :] * update).astype(jnp.bfloat16)
+        t_send[pl.ds(8 * n, 8)] = after.reshape(8, 16, 1152)
+        moves = []
+        for dz in (2, 1, 3, 0):
+            for to_y in (2 * n, 2 * n + 1):
+                to_z = turn(zlo, dz, 4)
+                move = Move(
+                    t_send.at[4 * to_y + to_z], t_recv.at[frame], (4 * to_z + to_y, patch), None, "there", "there"
+                )
+                if dz == 0:
+                    pl.when(y != to_y)(move.start)
+                else:
+                    move.start()
+                moves.append(move)
+        return moves
+
+    first = heads_back(0)
+    second = heads_back(1)
     for step in TAIL:
         steps[step[0]](*step[1:])
     wso_ring.done()
-    o_moves[0].wait_recv(o_recv.at[0:7])
-    update = dot(o_recv[...].reshape(1152, 256), wso[...].reshape(1152, 1152), 0, 0)
-    after = (hid_ref[...].astype(jnp.float32) + mod_s_ref[2:3, :] * update).astype(jnp.bfloat16)
-    t_send[...] = after.reshape(16, 16, 1152)
-
-    there = []
-    for d in range(1, 16):
-        to = turn(frame, d, 16)
-        there.append(Move(t_send.at[to], t_recv.at[frame], (to, patch), None, "there", "there"))
-    start(*there)
-    t_recv[frame] = t_send[frame]
+    there = spatial_end(0, first)
+    spatial_end(1, second)
+
+    t_recv[frame] = t_send[my_rows]
+    for step in LATE:
+        steps[step[0]](*step[1:])
     y_rings[0].sib[0].wait_recv(wt.at[0:15, 0])
     for pair in range(8):
         rows = [wt[2 * pair + k].reshape(288, 1152)[208:288].astype(jnp.float32)[8:80] for k in range(2)]
@@ -358,9 +385,9 @@
     back = []
     for d in range(1, 16):
         to = turn(frame, d, 16)
-        back.append(Move(r_send.at[to], out_ref.at[frame], (to, patch), None, "back", "back"))
+        back.append(Move(r_send.at[to], out_ref.at[my_rows], (to, patch), None, "back", "back"))
     start(*back)
-    out_ref[frame] = r_send[frame]
+    out_ref[my_rows] = r_send[frame]
     back[0].wait_recv(out_ref.at[0:15])
 
     sent("near", tok_b.at[0:4, 0:7])
@@ -371,7 +398,7 @@
     sent("zw", wso.at[0:3])
     sent("y", wt.at[0:6])
     sent("ysib", wt.at[0:15, 0])
-    sent("o", o_recv.at[0:7])
+    sent("o", o_recv.at[0:2, 0:7])
     sent("there", t_recv.at[0:15])
     sent("back", t_recv.at[0:15])
 
@@ -403,8 +430,8 @@
             pltpu.VMEM((2, 80, 4096), bf),
             pltpu.VMEM((2, 80, 2048), f32),
             pltpu.VMEM((2, 8, 2048), f32),
-            pltpu.VMEM((8, 144, 256), bf),
-            pltpu.VMEM((8, 144, 256), bf),
+            pltpu.VMEM((2, 8, 144, 128), bf),
+            pltpu.VMEM((2, 8, 144, 128), bf),
             pltpu.VMEM((16, 16, 1152), bf),
             pltpu.VMEM((16, 16, 1152), bf),
             pltpu.VMEM((16, 16, 1152), bf),

time: 139 us -> 132 us (0.950); the launches traced: 138 us -> 129 us
  Pallas kernels: 137 us -> 128 us
    pallas_call x1, Pallas kernels: 137 us -> 128 us  [shards(): pl.pallas_call(kernel, out_shape=jax.ShapeDtypeStruct((16, 16, 1152), bf)...]
where the time goes in v1:
time: 132 us; the launch traced here: 129 us
  Pallas kernels  128 us (97%)
  local copies, waits for them, and re-layouts  1.92 us (1%)
    pallas_call x1, Pallas kernels, shards(): pl.pallas_call(kernel, out_shape=jax.ShapeDtypeStruct((16, 16, 1152), bf)...  128 us

profile of v1, /device:TPU:32, one launch (start us, length us, event | category | flops | bytes accessed | tf_op | source)
XLA Modules:
  0.0 129.5 jit_solution(10193106674332948881)
XLA Ops:
  0.0 127.5 %st_block.1 = bf16[16,16,1152]{2,1,0:T(8,128)(2,1)} custom-call(bf16[256,1152]{1,0:T(8,128)(2,1)} %bitcast.5, f32[3,1152]{1,0:T(4,128)} %mod_s_ref.1, f32[3,1152]{1,0:T(4,128)} %mod_t_ref.1, bf16[216,1152]{1,0:T(8,128)(2,1)} %bitcast.6, bf16[72,1152]{1,0:T(8,128)(2,1)} %ws_out_ref.1, bf16[216,1152]{1,0:T(8,128)(2,1)} %bitcast.7, bf16[72,1152]{1,0:T(8,128)(2,1)} %wt_out_ref.1), custom_call_target="tpu_custom_call" | custom-call | tf_op jit(solution)/shard_map/st_block/pallas_call | solution.py:416
  127.5 1.9 %copy.9 = bf16[1,256,1152]{2,1,0:T(8,128)(2,1)} copy(bf16[1,256,1152]{2,1,0:T(8,128)(2,1)} %bitcast.4) | data formatting | bytes 1179648

commit v2 on v1

--- a/solution.py
+++ b/solution.py
@@ -351,10 +351,6 @@
     t_recv[frame] = t_send[my_rows]
     for step in LATE:
         steps[step[0]](*step[1:])
-    y_rings[0].sib[0].wait_recv(wt.at[0:15, 0])
-    for pair in range(8):
-        rows = [wt[2 * pair + k].reshape(288, 1152)[208:288].astype(jnp.float32)[8:80] for k in range(2)]
-        wto[pair] = jnp.concatenate(rows, axis=0).astype(jnp.bfloat16)
     there[0].wait_recv(t_recv.at[0:15])
     tokens = t_recv[...].reshape(256, 1152)
     t_moved = modulate(tokens, mod_t_ref)
@@ -364,7 +360,12 @@
     one = jnp.where(lax.broadcasted_iota(jnp.int32, (8, 256), 0) == 0, 1.0, 0.0)
     moved_t[...] = t_moved.astype(f32).T.astype(jnp.bfloat16)
 
+    y_rings[0].sib[0].wait_recv(wt.at[0:15, 0])
+
     def four_heads(g, _):
+        for j in range(2):
+            rows = [wt[4 * g + 2 * j + k].reshape(288, 1152)[208:288].astype(f32)[8:80] for k in range(2)]
+            wto[2 * g + j] = jnp.concatenate(rows, axis=0).astype(jnp.bfloat16)
         qkv = dot(wt[pl.ds(4 * g, 4)].reshape(1152, 1152), moved_t[...], 1, 0)
         for i in range(4):
             part = qkv[288 * i:288 * i + 216]

time: 132 us -> 131 us (level)
  no operation moved by 1% of the time
where the time goes in v2:
time: 131 us; the launch traced here: 130 us
  Pallas kernels  128 us (98%)
  local copies, waits for them, and re-layouts  1.92 us (1%)
    pallas_call x1, Pallas kernels, shards(): pl.pallas_call(kernel, out_shape=jax.ShapeDtypeStruct((16, 16, 1152), bf)...  128 us

profile of v2, /device:TPU:32, one launch (start us, length us, event | category | flops | bytes accessed | tf_op | source)
XLA Modules:
  0.0 129.5 jit_solution(5128289168074023376)
XLA Ops:
  0.0 127.6 %st_block.1 = bf16[16,16,1152]{2,1,0:T(8,128)(2,1)} custom-call(bf16[256,1152]{1,0:T(8,128)(2,1)} %bitcast.5, f32[3,1152]{1,0:T(4,128)} %mod_s_ref.1, f32[3,1152]{1,0:T(4,128)} %mod_t_ref.1, bf16[216,1152]{1,0:T(8,128)(2,1)} %bitcast.6, bf16[72,1152]{1,0:T(8,128)(2,1)} %ws_out_ref.1, bf16[216,1152]{1,0:T(8,128)(2,1)} %bitcast.7, bf16[72,1152]{1,0:T(8,128)(2,1)} %wt_out_ref.1), custom_call_target="tpu_custom_call" | custom-call | tf_op jit(solution)/shard_map/st_block/pallas_call | solution.py:417
  127.6 1.9 %copy.9 = bf16[1,256,1152]{2,1,0:T(8,128)(2,1)} copy(bf16[1,256,1152]{2,1,0:T(8,128)(2,1)} %bitcast.4) | data formatting | bytes 1179648
